TPU v7x, 256 devices: a whole 4x4x8 slice. The times are simulated.
256 devices in a mesh: group: 16 (over y, z_lo, core), fsdp: 16 (over z_hi, x).
Axes of the slice: x: 4, y: 4, z: 8 (z_hi: 4, z_lo: 2; z = z_hi * 2 + z_lo), core: 2. Of those that a mesh axis runs over, the one named last changes fastest.
Arguments:
- inputs: bfloat16 [16, 4096, 8192], P('group', 'fsdp'), may hold values from -6 to 6
- cotangent: bfloat16 [16, 4096, 512], P('group', 'fsdp'), may hold values from -0.29882812 to 0.29882812
- weight: bfloat16 [16, 8192, 512], P('group', 'fsdp'), may hold values from -6 to 6
- moment: bfloat16 [16, 8192, 512], P('group', 'fsdp'), may hold values from -6 to 6
- second: float32 [16, 8192, 512], P('group', 'fsdp'), may hold values from 0.5 to 4
- step_index: int32 [1], replicated, may hold values from 0 to 999
Outputs:
- input_grad: bfloat16 [16, 4096, 8192], P('group', 'fsdp')
- new_weight: bfloat16 [16, 8192, 512], P('group', 'fsdp')
- new_moment: bfloat16 [16, 8192, 512], P('group', 'fsdp')
- new_second: float32 [16, 8192, 512], P('group', 'fsdp')
All inputs are finite; a program needn't handle non-finite values.
Results may differ from a plain program's by a relative error of at most 0.013.
Values may be sent and summed in bfloat16 or wider, within the bound.
No kernel may reach another device: no remote copies, remote signals or barrier semaphores. Data moves between devices by JAX's collectives and lax.ppermute only.
A program may use at most 128 MiB of HBM per device.

v0:
```python
from functools import partial

import jax
import jax.numpy as jnp
from jax import lax
from jax.sharding import PartitionSpec as P


def shortened(x):
    return jax.tree.map(lambda a: a.astype(jnp.bfloat16) if a.dtype == jnp.float32 else a, x)


def swapped(x, axis, apart):
    return lax.ppermute(x, axis, [(i, i ^ 1 << apart) for i in range(lax.axis_size(axis))])


def trade_rows(updated, bit):
    return jax.tree.map(
        lambda part, own: part.astype(own.dtype), swapped(shortened(updated), "group", bit), updated
    )


def local(inputs, cotangent, weight, moment, second, step_index):
    features = inputs[0]
    upstream = cotangent[0]
    rows_here = weight[0]
    input_grad = lax.dot_general(
        upstream,
        lax.all_gather(rows_here, "fsdp", axis=0, tiled=True),
        (((1,), (1,)), ((), ())),
        preferred_element_type=jnp.float32,
    ).astype(jnp.bfloat16)
    gradient = lax.psum_scatter(
        lax.dot_general(
            features, upstream, (((0,), (0,)), ((), ())), preferred_element_type=jnp.float32
        ).astype(jnp.bfloat16),
        "fsdp",
        scatter_dimension=0,
        tiled=True,
    ).astype(jnp.float32)
    first = 0.9 * moment[0].astype(jnp.float32) + 0.1 * gradient
    new_second = 0.95 * second[0] + 0.05 * gradient * gradient
    weight_f = rows_here.astype(jnp.float32)
    updated = (weight_f - 0.1 * (first / (jnp.sqrt(new_second) + 1e-08) + 1.0 * weight_f)).astype(
        jnp.bfloat16
    )
    nbits = lax.axis_size("group").bit_length() - 1
    branches = [partial(trade_rows, bit=which) for which in range(nbits)]
    chosen = jnp.mod(step_index[0], nbits)
    partner_rows = lax.switch(chosen, branches, updated)
    new_weight = ((updated.astype(jnp.float32) + partner_rows.astype(jnp.float32)) * 0.5).astype(
        jnp.bfloat16
    )
    return (input_grad[None], new_weight[None], first.astype(jnp.bfloat16)[None], new_second[None])


def solution(mesh):
    return jax.shard_map(
        local,
        mesh=mesh,
        in_specs=(
            P("group", "fsdp", None),
            P("group", "fsdp", None),
            P("group", "fsdp", None),
            P("group", "fsdp", None),
            P("group", "fsdp", None),
            P(),
        ),
        out_specs=(
            P("group", "fsdp", None),
            P("group", "fsdp", None),
            P("group", "fsdp", None),
            P("group", "fsdp", None),
        ),
        check_vma=False,
    )
```

profile of v0, /device:TPU:1, one launch (start us, length us, event | category | flops | bytes accessed | tf_op | source)
XLA Modules:
  0.0 276.1 jit_solution(5638342852073226254)
XLA Ops:
  7.2 0.0 copy-start
  7.2 0.0 all-gather.3.cloned.1.call-start
  7.2 0.7 all-gather.3.cloned.1.call-update
  7.9 0.0 reduce-scatter.2.cloned.1.call-start
  8.0 0.2 copy-done
  8.1 7.8 %convolution_convert_fusion = bf16[8192,512]{1,0:T(8,128)(2,1)} fusion(bf16[1,256,8192]{2,1,0:T(8,128)(2,1)} %param.10, bf16[1,256,512]{2,1,0:T(8,128)(2,1)S(1)} %copy-done), kind=kOutput, calls=%fused_computation | convolution fusion | flops 2151677952 | bytes 12845056 | tf_op jit(solution)/shard_map/dot_general | solution.py:34
  15.9 0.0 reduce-scatter.2.cloned.1.call-update
  15.9 0.0 copy-start.1
  16.0 0.0 copy-start.2
  16.0 0.0 copy-start.3
  16.8 108.5 %all-gather.3.cloned.1.call-done = bf16[1,8192,512]{2,1,0:T(8,128)(2,1)} async-done(((bf16[1,512,512]{2,1,0:T(8,128)(2,1)}), bf16[1,8192,512]{2,1,0:T(8,128)(2,1)}) %all-gather.3.cloned.1.call-update) | async-done | bytes 8388624 | tf_op jit(solution)/shard_map/all_gather | solution.py:29
  125.3 7.8 %fusion = bf16[1,256,8192]{2,1,0:T(8,128)(2,1)} fusion(bf16[1,8192,512]{2,1,0:T(8,128)(2,1)} %all-gather.3.cloned.1.call-done, bf16[1,256,512]{2,1,0:T(8,128)(2,1)S(1)} %copy-done), kind=kOutput, calls=%fused_computation.2 | convolution fusion | flops 2149580800 | bytes 12845056 | tf_op jit(solution)/shard_map/dot_general | solution.py:27
  133.0 119.4 %reduce-scatter.2.cloned.1.call-done = bf16[512,512]{1,0:T(8,128)(2,1)} async-done(((bf16[8192,512]{1,0:T(8,128)(2,1)}), bf16[512,512]{1,0:T(8,128)(2,1)}) %reduce-scatter.2.cloned.1.call-update) | async-done | bytes 524304 | tf_op jit(solution)/shard_map/reduce_scatter | solution.py:33
  252.5 0.0 copy-done.1
  252.5 0.0 copy-done.2
  252.5 0.0 copy-done.3
  252.5 3.0 %fusion.8 = (f32[1,512,512]{2,1,0:T(8,128)}, bf16[512,512]{1,0:T(8,128)(2,1)S(1)}, bf16[1,512,512]{2,1,0:T(8,128)(2,1)}) fusion(bf16[512,512]{1,0:T(8,128)(2,1)} %reduce-scatter.2.cloned.1.call-done, f32[1,512,512]{2,1,0:T(8,128)S(1)} %copy-done.2, bf16[1,512,512]{2,1,0:T(8,128)(2,1)S(1)} %copy-done.3, bf16[1,512,512]{2,1,0:T(8,128)(2,1)S(1)} %copy-done.1), kind=kLoop, calls=%fused_computation.15 | loop fusion | flops 4456448 | bytes 4718592 | tf_op jit(solution)/shard_map/broadcast_in_dim | solution.py:54
  255.5 11.8 %conditional.4 = (bf16[512,512]{1,0:T(8,128)(2,1)}) conditional(s32[]{:T(128)} %clamp.3, bf16[512,512]{1,0:T(8,128)(2,1)S(1)} %get-tuple-element.20, bf16[512,512]{1,0:T(8,128)(2,1)S(1)} %get-tuple-element.20, bf16[512,512]{1,0:T(8,128)(2,1)S(1)} %get-tuple-element.20, bf16[512,512]{1,0:T(8,128)(2,1)S(1)} %get-tuple-element.20), branch_computations={%region_1.2_spmd, %region_2.3_spmd, %region_3.4_spmd, %region_4.5_... | conditional | bytes 2097200
  255.5 1.5 collective-permute-start.1
  256.9 10.4 %collective-permute-done.1 = bf16[512,512]{1,0:T(8,128)(2,1)} collective-permute-done((bf16[512,512]{1,0:T(8,128)(2,1)S(1)}, bf16[512,512]{1,0:T(8,128)(2,1)}, u32[]{:S(2)}, u32[]{:S(2)}) %collective-permute-start.1) | collective-permute-done | bytes 524320 | tf_op jit(solution)/shard_map/cond/branch_1_fun/ppermute | solution.py:14
  267.3 2.0 fusion.10
Async XLA Ops:
  7.2 1.0 copy-start
  7.2 118.1 %all-gather.3.cloned.1.call-start = ((), (), s32[]{:S(2)}) async-start(), calls=%async_computation.2 | async-start | bytes 8912896 | tf_op jit(solution)/shard_map/all_gather | solution.py:29
  7.9 244.6 %reduce-scatter.2.cloned.1.call-start = ((), (), s32[]{:S(2)}) async-start(), calls=%async_computation.1 | async-start | bytes 8912896 | tf_op jit(solution)/shard_map/reduce_scatter | solution.py:33
  15.9 236.5 %copy-start.1 = (bf16[1,512,512]{2,1,0:T(8,128)(2,1)S(1)}, bf16[1,512,512]{2,1,0:T(8,128)(2,1)}, u32[]{:S(2)}) copy-start(bf16[1,512,512]{2,1,0:T(8,128)(2,1)} %param.12) | copy-start | bytes 1572868
  16.0 236.5 %copy-start.2 = (f32[1,512,512]{2,1,0:T(8,128)S(1)}, f32[1,512,512]{2,1,0:T(8,128)}, u32[]{:S(2)}) copy-start(f32[1,512,512]{2,1,0:T(8,128)} %param.14) | copy-start | bytes 3145732
  16.0 236.5 %copy-start.3 = (bf16[1,512,512]{2,1,0:T(8,128)(2,1)S(1)}, bf16[1,512,512]{2,1,0:T(8,128)(2,1)}, u32[]{:S(2)}) copy-start(bf16[1,512,512]{2,1,0:T(8,128)(2,1)} %param.13) | copy-start | bytes 1572868
  255.5 11.8 %collective-permute-start.1 = (bf16[512,512]{1,0:T(8,128)(2,1)S(1)}, bf16[512,512]{1,0:T(8,128)(2,1)}, u32[]{:S(2)}, u32[]{:S(2)}) collective-permute-start(bf16[512,512]{1,0:T(8,128)(2,1)S(1)} %param.1), channel_id=1, source_target_pairs={{0,32},{16,48},{32,0},{48,16},{64,96},{80,112},{96,64},{112,80},{1... | collective-permute-start | bytes 1572872 | tf_op jit(solution)/shard_map/cond/branch_1_fun/ppermute | solution.py:14
Sparse Core Ops, SparseCore 0:
  10.4 114.7 all-gather.2
  128.9 123.4 reduce-scatter.1
where the time goes:
time: 279 us; the launch traced here: 276 us
  waiting for transfers between devices  239 us (86%)
  matrix products  15.6 us (6%)
  between operations  14.9 us (5%)
  other arithmetic  4.98 us (2%)
    reduce_scatter x1, waiting for transfers between devices, local(): lax.psum_scatter(lax.dot_general(features, upstream, (((0,), (0,)), ((),...  119 us
    all_gather x1, waiting for transfers between devices, local(): lax.all_gather(rows_here, 'fsdp', axis=0, tiled=True)  108 us
    ppermute x1, waiting for transfers between devices, swapped(): lax.ppermute(x, axis, [(i, i ^ 1 << apart) for i in range(lax.axis_size(a...  10.4 us
    dot_general x1, matrix products, local(): lax.dot_general(features, upstream, (((0,), (0,)), ((), ())), preferred_e...  7.8 us
    dot_general x1, matrix products, local(): lax.dot_general(upstream, lax.all_gather(rows_here, 'fsdp', axis=0, tiled...  7.77 us
  transfers between devices with their start and end apart: 3, of which 3 were waited for; matrix products, arithmetic and copies ran while one was open for 6% of the time, Pallas kernels for 0%

commit v1 on v0

v1 whole, which is shorter than its diff:
```python
from functools import partial

import jax
import jax.numpy as jnp
from jax import lax
from jax.experimental import pallas as pl
from jax.experimental.pallas import tpu as pltpu
from jax.sharding import PartitionSpec as P

X = 4
Z = 4


def moved(v, along, flip=0):
    def target(g, f):
        z, x = f // X, f % X
        if along == "x":
            x = partners(g, x)[flip]
        else:
            z = (z + (1 if g % 2 == flip else 3)) % Z
        return z * X + x

    groups = lax.axis_size("group")
    pairs = [
        (g * X * Z + f, g * X * Z + target(g, f)) for g in range(groups) for f in range(X * Z)
    ]
    return lax.ppermute(v, ("group", "fsdp"), pairs)


def partners(g, x):
    ways = (x ^ 1, 3 - x)
    return ways if g % 2 == 0 else ways[::-1]


def swapped(v, bit):
    return lax.ppermute(
        v, "group", [(i, i ^ 1 << bit) for i in range(lax.axis_size("group"))]
    )


HERE_X, FIRST, SECOND, BOTH = 2, 3, 4, 5


def column(place_ref, zs, xs, depth):
    z, up = place_ref[0], place_ref[1]
    zs = {"up": up, "down": 4 - up}.get(zs, zs)
    block = lax.rem(z + zs, Z) * X + place_ref[xs]
    return pl.ds(pl.multiple_of(block * depth, depth), depth)


def carry(copies):
    for copy in copies:
        copy.start()
    for copy in copies:
        copy.wait()


def kernel_call(body, out_shapes, in_specs, out_specs, copies=0, aliases=None, cost=1):
    return pl.pallas_call(
        body,
        in_specs=in_specs,
        out_specs=out_specs,
        out_shape=out_shapes,
        scratch_shapes=[pltpu.SemaphoreType.DMA((copies,))] if copies else [],
        input_output_aliases=aliases or {},
        compiler_params=pltpu.CompilerParams(vmem_limit_bytes=16 << 20),
        cost_estimate=pl.CostEstimate(flops=cost, bytes_accessed=cost, transcendentals=0),
    )


SCALARS = pl.BlockSpec(memory_space=pltpu.SMEM)
THERE = pl.BlockSpec(memory_space=pl.ANY)
HERE = pl.BlockSpec(memory_space=pltpu.VMEM)


def pick_kernel(blocks, place_ref, whole_ref, *refs):
    *tails, out_ref, sems = refs
    depth = out_ref.shape[1]
    tokens = whole_ref.shape[0]
    sources = [whole_ref.at[:, column(place_ref, *b, depth)] for b in blocks] + tails
    carry(
        [
            pltpu.make_async_copy(src, out_ref.at[n * tokens : (n + 1) * tokens], sems.at[n])
            for n, src in enumerate(sources)
        ]
    )


def picked(place, blocks, whole, *tails, cost=1):
    tokens, width = whole.shape
    count = len(blocks) + len(tails)
    return kernel_call(
        partial(pick_kernel, blocks),
        jax.ShapeDtypeStruct((count * tokens, width // (X * Z)), whole.dtype),
        [SCALARS] + [THERE] * (1 + len(tails)),
        HERE,
        copies=count,
        cost=cost,
    )(place, whole, *tails)


def placing(blocks, place_ref, parts, out_ref, sems):
    tokens, depth = out_ref.shape[0], parts[0].shape[1]
    copies = []
    for part_ref, some in zip(parts, blocks):
        for n, b in enumerate(some):
            copies.append(
                pltpu.make_async_copy(
                    part_ref.at[n * tokens : (n + 1) * tokens],
                    out_ref.at[:, column(place_ref, *b, depth)],
                    sems.at[len(copies)],
                )
            )
    return copies


def place_kernel(blocks, place_ref, *refs):
    parts, (out_ref, sems) = refs[: len(blocks)], refs[-2:]
    carry(placing(blocks, place_ref, parts, out_ref, sems))


def placed(place, parts, blocks, width, whole=()):
    return kernel_call(
        partial(place_kernel, blocks),
        jax.ShapeDtypeStruct((parts[0].shape[0] // len(blocks[0]), width), parts[0].dtype),
        [SCALARS] + [HERE] * len(parts) + [THERE] * len(whole),
        THERE,
        copies=sum(map(len, blocks)),
        aliases={1 + len(parts): 0} if whole else None,
    )(place, *parts, *whole)


def product_kernel(a_ref, b_ref, u_ref, v_ref, *out_refs):
    tokens = u_ref.shape[0] // 5
    for n, out_ref in enumerate(out_refs):
        total = 0.0
        for p, w in ((a_ref, u_ref), (b_ref, v_ref)):
            total += lax.dot_general(
                p[n * tokens : (n + 1) * tokens],
                w[4 * tokens :],
                (((0,), (0,)), ((), ())),
                preferred_element_type=jnp.float32,
            )
        out_ref[...] = total.astype(out_ref.dtype)


def products(own, came, own_first, came_first):
    depth, outs = own.shape[1], own_first.shape[1]
    return kernel_call(
        product_kernel,
        tuple(jax.ShapeDtypeStruct((depth, outs), t) for t in (jnp.float32, jnp.bfloat16) * 2),
        [HERE] * 4,
        (HERE,) * 4,
    )(own, came, own_first, came_first)


def rows_kernel(u_ref, v_ref, *refs):
    *weights, out_ref, own_ref = refs
    tokens = u_ref.shape[0] // 5
    for first_ref, to_ref in ((u_ref, out_ref), (v_ref, own_ref)):
        for n, w in enumerate(weights):
            to_ref[n * tokens : (n + 1) * tokens] = lax.dot_general(
                first_ref[4 * tokens :],
                w[...],
                (((1,), (1,)), ((), ())),
                preferred_element_type=jnp.float32,
            ).astype(to_ref.dtype)


def rows_times(first, own_first, *weights):
    tokens, depth = first.shape[0] // 5, first.shape[1]
    out = jax.ShapeDtypeStruct((tokens * len(weights), depth), first.dtype)
    return kernel_call(rows_kernel, (out, out), [HERE] * (2 + len(weights)), (HERE, HERE))(
        first, own_first, *weights
    )


class Line:
    def __init__(self):
        self.last = ()

    def __call__(self, *values):
        values, self.last = lax.optimization_barrier((values, self.last))
        self.last = values[:1]
        return values[0] if len(values) == 1 else values

    def run(self, f, *values):
        out = f(*lax.optimization_barrier((values, self.last))[0])
        self.last = (out[0] if isinstance(out, tuple) else out,)
        return out


def local(inputs, cotangent, weight, moment, second, step_index):
    features = inputs[0]
    upstream = cotangent[0]
    rows_here = weight[0]
    tokens, width = features.shape
    depth, outs = rows_here.shape
    me = lax.axis_index("fsdp")
    z, x = me // X, me % X
    odd = lax.axis_index("group") % 2
    one_way, other_way = x ^ 1, 3 - x
    place = [z, 1 + 2 * odd, x]
    place += [jnp.where(odd == 0, one_way, other_way), jnp.where(odd == 0, other_way, one_way)]
    place = jnp.stack(place + [x ^ 2]).astype(jnp.int32)
    line = Line()
    run = line.run

    def first_part(*ways):
        blocks = [(r, w) for r in (2, "up") for w in ways]
        return run(lambda f, u: picked(place, blocks, f, u), features, upstream)

    def second_part(*ways, cost=1):
        blocks = [(r, w) for r in ("down", 0) for w in ways]
        return run(lambda f: picked(place, blocks, f, cost=cost), features)

    def long(v):
        return v.astype(jnp.float32)

    def put(parts, whole=()):
        blocks = [[(r, x) for r in zs] for _, zs, x in parts]
        n = len(parts)
        return [
            run(
                lambda *p: placed(place, p[:n], blocks, width, p[n:]),
                *[part for part, _, _ in parts],
                *whole,
            )
        ]

    def added(a, *v):
        return sum(map(long, v), a).astype(jnp.bfloat16)

    def queued(v):
        return run(lambda w: w, v)

    near, rest = (0, "up"), ("down", 2)

    above = moved(rows_here, "z", 1)
    below = moved(rows_here, "z", 0)
    first = moved(first_part(FIRST, BOTH), "x")
    second_in = moved(second_part(FIRST, BOTH), "x")
    own_first = first_part(HERE_X, SECOND)
    above = line(above)
    below = line(below)
    across = moved(queued(above), "z", 1)
    own_second = second_part(HERE_X, SECOND, cost=10**11)
    first = line(first)
    far, give_far, up, give_up = run(lambda a, b: products(a, b, a, b), own_first, first)
    give_far = moved(give_far, "x", 1)
    give_up = moved(give_up, "x", 1)
    out_near, own_near = run(rows_times, first, own_first, rows_here, above)
    out_near = moved(out_near, "x")
    give_far = line(give_far)
    far = moved(run(added, far, give_far), "z", 0)
    second_in = line(second_in)
    down, give_down, own, give_own = run(products, own_second, second_in, own_first, first)
    give_down = moved(give_down, "x", 1)
    across = line(across)
    give_own = moved(give_own, "x", 1)
    give_up = line(give_up)
    there = moved(rows_here, "x", 1)
    out_rest, own_rest = run(rows_times, first, own_first, below, across)
    out_near = line(out_near)
    there_above = moved(above, "x", 1)
    input_grad = put(
        [(own_near, near, HERE_X), (own_rest, rest, HERE_X), (out_near, near, FIRST)]
    )
    give_down = line(give_down)
    near_down = moved(run(added, down, give_down), "z", 1)
    give_own = line(give_own)
    far = line(far)
    near_up = moved(run(added, up, give_up, far), "z", 0)
    there_below = moved(below, "x", 1)
    there = line(there)
    there_across = moved(across, "x", 1)
    there_above = line(there_above)
    more_near, own_more_near = run(rows_times, first, own_first, there, there_above)
    input_grad = put([(own_more_near, near, SECOND)], input_grad)
    there_below = line(there_below)
    there_across = line(there_across)
    out_rest = moved(queued(out_rest), "x")
    more_near = moved(queued(more_near), "x")
    more_rest, own_more_rest = run(
        rows_times, first, own_first, there_below, there_across
    )
    more_rest = moved(more_rest, "x")
    near_up = line(near_up)
    near_down = line(near_down)
    gradient = own + long(give_own) + long(near_up) + long(near_down)
    new_moment = 0.9 * moment[0].astype(jnp.float32) + 0.1 * gradient
    new_second = 0.95 * second[0] + 0.05 * gradient * gradient
    weight_f = rows_here.astype(jnp.float32)
    updated = (
        weight_f - 0.1 * (new_moment / (jnp.sqrt(new_second) + 1e-08) + 1.0 * weight_f)
    ).astype(jnp.bfloat16)
    new_moment = new_moment.astype(jnp.bfloat16)
    nbits = lax.axis_size("group").bit_length() - 1
    chosen = jnp.mod(step_index[0], nbits)
    partner_rows = lax.switch(chosen, [partial(swapped, bit=b) for b in range(nbits)], updated)
    partner_rows = line(partner_rows)
    new_weight = ((updated.astype(jnp.float32) + partner_rows.astype(jnp.float32)) * 0.5).astype(
        jnp.bfloat16
    )
    new_weight = line(new_weight)
    out_rest, more_near, more_rest = line(out_rest, more_near, more_rest)
    input_grad = put(
        [
            (own_more_rest, rest, SECOND),
            (out_rest, rest, FIRST),
            (more_near, near, BOTH),
            (more_rest, rest, BOTH),
        ],
        input_grad,
    )[0]
    return (input_grad[None], new_weight[None], new_moment[None], new_second[None])


def solution(mesh):
    sharded = P("group", "fsdp", None)
    return jax.shard_map(
        local,
        mesh=mesh,
        in_specs=(sharded,) * 5 + (P(),),
        out_specs=(sharded,) * 4,
        check_vma=False,
    )
```

time: 279 us -> 123 us (0.44)
  waiting for transfers between devices: 239 us -> 49.8 us
  starting transfers between devices: 1.55 us -> 37.1 us
  Pallas kernels: 0 us -> 20.1 us
  matrix products: 15.6 us -> 0 us
  between operations: 14.9 us -> 1.67 us
  local copies, waits for them, and re-layouts: 0.19 us -> 5.89 us
  other arithmetic: 4.98 us -> 8.3 us
    reduce_scatter x1 -> x0, waiting for transfers between devices: 119 us -> none  [local(): lax.psum_scatter(lax.dot_general(features, upstream, (((0,), (0,)), ((),...]
    all_gather x1 -> x0, waiting for transfers between devices: 108 us -> none  [local(): lax.all_gather(rows_here, 'fsdp', axis=0, tiled=True)]
    ppermute x1 -> x21, waiting for transfers between devices: 10.4 us -> 49.8 us  [the longest x20 37.6 us: moved(): return lax.ppermute(v, ('group', 'fsdp'), pairs)]
    ppermute x1 -> x21, starting transfers between devices: 1.48 us -> 37.1 us  [the longest x20 35.6 us: moved(): return lax.ppermute(v, ('group', 'fsdp'), pairs)]
    pallas_call x0 -> x13, Pallas kernels: none -> 20.1 us  [the longest x4 9.08 us: rows_times(): kernel_call(rows_kernel, (out, out), [HERE] * (2 + len(weights)), (HERE,...]
    dot_general x2 -> x0, matrix products: 15.6 us -> none  [the longest x1 7.8 us: local(): lax.dot_general(features, upstream, (((0,), (0,)), ((), ())), preferred_e...]
    unnamed x8 -> x28, local copies, waits for them, and re-layouts: 0.19 us -> 5.8 us
    convert_element_type x0 -> x4, other arithmetic: none -> 4.15 us  [the longest x3 2.16 us: added(): return sum(map(long, v), a).astype(jnp.bfloat16)]
  transfers between devices with their start and end apart: 3 -> 21, of which waited for: 3 -> 9; matrix products, arithmetic and copies ran while one was open for 6% -> 7% of each run, Pallas kernels for 0% -> 14%
where the time goes in v1:
time: 123 us
  waiting for transfers between devices  49.8 us (40%)
  starting transfers between devices  37.1 us (30%)
  Pallas kernels  20.1 us (16%)
  other arithmetic  8.3 us (7%)
  local copies, waits for them, and re-layouts  5.89 us (5%)
  between operations  1.67 us (1%)
    ppermute x20, waiting for transfers between devices, moved(): return lax.ppermute(v, ('group', 'fsdp'), pairs)  37.6 us
    ppermute x20, starting transfers between devices, moved(): return lax.ppermute(v, ('group', 'fsdp'), pairs)  35.6 us
    ppermute x1, waiting for transfers between devices, swapped(): lax.ppermute(v, 'group', [(i, i ^ 1 << bit) for i in range(lax.axis_size(...  12.2 us
    pallas_call x4, Pallas kernels, rows_times(): kernel_call(rows_kernel, (out, out), [HERE] * (2 + len(weights)), (HERE,...  9.08 us
    unnamed x28, local copies, waits for them, and re-layouts  5.8 us
    pallas_call x3, Pallas kernels, placed(): kernel_call(partial(place_kernel, blocks), jax.ShapeDtypeStruct((parts[0]...  5.68 us
    pallas_call x4, Pallas kernels, picked(): kernel_call(partial(pick_kernel, blocks), jax.ShapeDtypeStruct((count * t...  2.75 us
    broadcast_in_dim x1, other arithmetic, local(): new_second[None]  2.58 us
  transfers between devices with their start and end apart: 21, of which 9 were waited for; matrix products, arithmetic and copies ran while one was open for 7% of the time, Pallas kernels for 14%

profile of v1, /device:TPU:1, one launch (start us, length us, event | category | flops | bytes accessed | tf_op | source)
XLA Modules:
  0.0 122.8 jit_solution(13238894503926354378)
XLA Ops:
  0.6 3.9 %collective-permute-start.5 = (bf16[512,512]{1,0:T(8,128)(2,1)}, bf16[512,512]{1,0:T(8,128)(2,1)}, u32[]{:S(2)}, u32[]{:S(2)}) collective-permute-start(bf16[512,512]{1,0:T(8,128)(2,1)} %bitcast.38), channel_id=1, source_target_pairs={{0,12},{1,13},{2,14},{3,15},{4,0},{5,1},{6,2},{7,3},{8,4},{9,5},{1... | collective-permute-start | bytes 1572872 | tf_op jit(solution)/shard_map/ppermute | solution.py:27
  4.5 3.1 %collective-permute-start.6 = (bf16[512,512]{1,0:T(8,128)(2,1)}, bf16[512,512]{1,0:T(8,128)(2,1)}, u32[]{:S(2)}, u32[]{:S(2)}) collective-permute-start(bf16[512,512]{1,0:T(8,128)(2,1)} %bitcast.39), channel_id=1, source_target_pairs={{0,4},{1,5},{2,6},{3,7},{4,8},{5,9},{6,10},{7,11},{8,12},{9,13},{1... | collective-permute-start | bytes 1572872 | tf_op jit(solution)/shard_map/ppermute | solution.py:27
  7.7 2.2 %copy-done = bf16[1,256,8192]{2,1,0:T(8,128)(2,1)S(1)} copy-done((bf16[1,256,8192]{2,1,0:T(8,128)(2,1)S(1)}, bf16[1,256,8192]{2,1,0:T(8,128)(2,1)}, u32[]{:S(2)}) %copy-start) | copy-done | bytes 4194328
  11.6 2.6 %collective-permute-start.4 = (bf16[1280,512]{1,0:T(8,128)(2,1)S(1)}, bf16[1280,512]{1,0:T(8,128)(2,1)S(1)}, u32[]{:S(2)}, u32[]{:S(2)}) collective-permute-start(bf16[1280,512]{1,0:T(8,128)(2,1)S(1)} %shard_map.93), channel_id=1, source_target_pairs={{0,1},{1,0},{2,3},{3,2},{4,5},{5,4},{6,7},{7,6},{8,9},{9,8},{10,11... | collective-permute-start | bytes 3932168 | tf_op jit(solution)/shard_map/ppermute | solution.py:27
  15.8 3.8 %collective-permute-done.5.refs_1_ = bf16[512,512]{1,0:T(8,128)(2,1)} collective-permute-done((bf16[512,512]{1,0:T(8,128)(2,1)}, bf16[512,512]{1,0:T(8,128)(2,1)}, u32[]{:S(2)}, u32[]{:S(2)}) %collective-permute-start.5) | collective-permute-done | bytes 524320 | tf_op jit(solution)/shard_map/ppermute | solution.py:27
  19.6 11.1 %collective-permute-done.6.refs_0_ = bf16[512,512]{1,0:T(8,128)(2,1)} collective-permute-done((bf16[512,512]{1,0:T(8,128)(2,1)}, bf16[512,512]{1,0:T(8,128)(2,1)}, u32[]{:S(2)}, u32[]{:S(2)}) %collective-permute-start.6) | collective-permute-done | bytes 524320 | tf_op jit(solution)/shard_map/ppermute | solution.py:27
  32.8 3.8 %collective-permute-start.10 = (bf16[512,512]{1,0:T(8,128)(2,1)}, bf16[512,512]{1,0:T(8,128)(2,1)}, u32[]{:S(2)}, u32[]{:S(2)}) collective-permute-start(bf16[512,512]{1,0:T(8,128)(2,1)} %collective-permute-done.5.refs_1_), channel_id=1, source_target_pairs={{0,12},{1,13},{2,14},{3,15},{4,0},{5,1},{6,2},{7,3},{8,4},{9,5},{1... | collective-permute-start | bytes 1572872 | tf_op jit(solution)/shard_map/ppermute | solution.py:27
  38.7 2.6 %collective-permute-start.16 = (bf16[512,512]{1,0:T(8,128)(2,1)S(1)}, bf16[512,512]{1,0:T(8,128)(2,1)S(1)}, u32[]{:S(2)}, u32[]{:S(2)}) collective-permute-start(bf16[512,512]{1,0:T(8,128)(2,1)S(1)} %get-tuple-element.119), channel_id=1, source_target_pairs={{0,1},{1,0},{2,3},{3,2},{4,5},{5,4},{6,7},{7,6},{8,9},{9,8},{10,11... | collective-permute-start | bytes 1572872 | tf_op jit(solution)/shard_map/ppermute | solution.py:27
  41.2 5.7 %collective-permute-done.12 = bf16[512,512]{1,0:T(8,128)(2,1)S(1)} collective-permute-done((bf16[512,512]{1,0:T(8,128)(2,1)S(1)}, bf16[512,512]{1,0:T(8,128)(2,1)S(1)}, u32[]{:S(2)}, u32[]{:S(2)}) %collective-permute-start.12) | collective-permute-done | bytes 524320 | tf_op jit(solution)/shard_map/ppermute | solution.py:27
  50.0 3.8 %collective-permute-start.13 = (bf16[512,512]{1,0:T(8,128)(2,1)S(1)}, bf16[512,512]{1,0:T(8,128)(2,1)S(1)}, u32[]{:S(2)}, u32[]{:S(2)}) collective-permute-start(bf16[512,512]{1,0:T(8,128)(2,1)S(1)} %add_convert_fusion.2), channel_id=1, source_target_pairs={{0,4},{1,5},{2,6},{3,7},{4,8},{5,9},{6,10},{7,11},{8,12},{9,13},{1... | collective-permute-start | bytes 1572872 | tf_op jit(solution)/shard_map/ppermute | solution.py:27
  53.8 4.1 %collective-permute-done.9 = bf16[512,512]{1,0:T(8,128)(2,1)S(1)} collective-permute-done((bf16[512,512]{1,0:T(8,128)(2,1)S(1)}, bf16[512,512]{1,0:T(8,128)(2,1)S(1)}, u32[]{:S(2)}, u32[]{:S(2)}) %collective-permute-start.9) | collective-permute-done | bytes 524320 | tf_op jit(solution)/shard_map/ppermute | solution.py:27
  58.1 2.5 %shard_map.100 = (bf16[512,512]{1,0:T(8,128)(2,1)}, bf16[512,512]{1,0:T(8,128)(2,1)S(1)}) custom-call(bf16[1280,512]{1,0:T(8,128)(2,1)S(1)} %collective-permute-done.4.b_ref.v_ref.u_ref, bf16[1280,512]{1,0:T(8,128)(2,1)S(1)} %shard_map.95.a_ref.u_ref.v_ref, bf16[512,512]{1,0:T(8,128)(2,1)} %collective-permute-done.6.refs_0_, ...), custom_call_target="tpu_custom_call" | custom-call | flops 1 | bytes 1 | tf_op jit(solution)/shard_map/pallas_call | solution.py:173
  65.6 3.5 %collective-permute-done.14 = bf16[512,512]{1,0:T(8,128)(2,1)S(1)} collective-permute-done((bf16[512,512]{1,0:T(8,128)(2,1)S(1)}, bf16[512,512]{1,0:T(8,128)(2,1)S(1)}, u32[]{:S(2)}, u32[]{:S(2)}) %collective-permute-start.14) | collective-permute-done | bytes 524320 | tf_op jit(solution)/shard_map/ppermute | solution.py:27
  71.3 3.9 %collective-permute-start.22 = (bf16[512,512]{1,0:T(8,128)(2,1)}, bf16[512,512]{1,0:T(8,128)(2,1)}, u32[]{:S(2)}, u32[]{:S(2)}) collective-permute-start(bf16[512,512]{1,0:T(8,128)(2,1)} %add_convert_fusion), channel_id=1, source_target_pairs={{0,4},{1,5},{2,6},{3,7},{4,8},{5,9},{6,10},{7,11},{8,12},{9,13},{1... | collective-permute-start | bytes 1572872 | tf_op jit(solution)/shard_map/ppermute | solution.py:27
  77.5 2.9 %collective-permute-done.17.refs_1_ = bf16[512,512]{1,0:T(8,128)(2,1)} collective-permute-done((bf16[512,512]{1,0:T(8,128)(2,1)}, bf16[512,512]{1,0:T(8,128)(2,1)}, u32[]{:S(2)}, u32[]{:S(2)}) %collective-permute-start.17) | collective-permute-done | bytes 524320 | tf_op jit(solution)/shard_map/ppermute | solution.py:27
  81.5 2.3 %shard_map.102 = (bf16[512,512]{1,0:T(8,128)(2,1)}, bf16[512,512]{1,0:T(8,128)(2,1)S(1)}) custom-call(bf16[1280,512]{1,0:T(8,128)(2,1)S(1)} %collective-permute-done.4.b_ref.v_ref.u_ref, bf16[1280,512]{1,0:T(8,128)(2,1)S(1)} %shard_map.95.a_ref.u_ref.v_ref, bf16[512,512]{1,0:T(8,128)(2,1)S(1)} %copy-done.7, bf16[512,512]{1,0:T(8,128)(2,1)} %collective-permute-done.17.refs_1_), custom_call_target="tpu_custom_call" | custom-call | flops 1 | bytes 1 | tf_op jit(solution)/shard_map/pallas_call | solution.py:173
  86.0 5.6 %collective-permute-done.18.refs_1_ = bf16[512,512]{1,0:T(8,128)(2,1)} collective-permute-done((bf16[512,512]{1,0:T(8,128)(2,1)}, bf16[512,512]{1,0:T(8,128)(2,1)}, u32[]{:S(2)}, u32[]{:S(2)}) %collective-permute-start.18) | collective-permute-done | bytes 524320 | tf_op jit(solution)/shard_map/ppermute | solution.py:27
  91.7 2.5 %collective-permute-start.20 = (bf16[512,512]{1,0:T(8,128)(2,1)}, bf16[512,512]{1,0:T(8,128)(2,1)}, u32[]{:S(2)}, u32[]{:S(2)}) collective-permute-start(bf16[512,512]{1,0:T(8,128)(2,1)} %get-tuple-element.165), channel_id=1, source_target_pairs={{0,1},{1,0},{2,3},{3,2},{4,5},{5,4},{6,7},{7,6},{8,9},{9,8},{10,11... | collective-permute-start | bytes 1572872 | tf_op jit(solution)/shard_map/ppermute | solution.py:27
  94.3 2.5 %shard_map.104 = (bf16[512,512]{1,0:T(8,128)(2,1)}, bf16[512,512]{1,0:T(8,128)(2,1)S(1)}) custom-call(bf16[1280,512]{1,0:T(8,128)(2,1)S(1)} %collective-permute-done.4.b_ref.v_ref.u_ref, bf16[1280,512]{1,0:T(8,128)(2,1)S(1)} %shard_map.95.a_ref.u_ref.v_ref, bf16[512,512]{1,0:T(8,128)(2,1)} %collective-permute-done.7.refs_0_, ...), custom_call_target="tpu_custom_call" | custom-call | flops 1 | bytes 1 | tf_op jit(solution)/shard_map/pallas_call | solution.py:173
  97.6 2.5 %collective-permute-start.21 = (bf16[512,512]{1,0:T(8,128)(2,1)}, bf16[512,512]{1,0:T(8,128)(2,1)S(1)}, u32[]{:S(2)}, u32[]{:S(2)}) collective-permute-start(bf16[512,512]{1,0:T(8,128)(2,1)} %get-tuple-element.171), channel_id=1, source_target_pairs={{0,1},{1,0},{2,3},{3,2},{4,5},{5,4},{6,7},{7,6},{8,9},{9,8},{10,11... | collective-permute-start | bytes 1572872 | tf_op jit(solution)/shard_map/ppermute | solution.py:27
  100.1 2.6 %fusion.5 = (f32[1,512,512]{2,1,0:T(8,128)}, f32[512,512]{1,0:T(8,128)S(1)}) fusion(f32[1,512,512]{2,1,0:T(8,128)S(1)} %copy-done.10, bf16[512,512]{1,0:T(8,128)(2,1)} %collective-permute-done.23, bf16[512,512]{1,0:T(8,128)(2,1)} %collective-permute-done.22, f32[512,512]{1,0:T(8,128)S(1)} %copy-done.5, bf16[512,512]{1,0:T(8,128)(2,1)S(1)} %copy-done.13), kind=kLoop, calls=%fused_computation.14 | loop fusion | flops 2621440 | bytes 5767168 | tf_op jit(solution)/shard_map/broadcast_in_dim | solution.py:316
  104.3 13.8 %conditional.1 = (bf16[512,512]{1,0:T(8,128)(2,1)}) conditional(s32[]{:T(128)} %clamp.3, bf16[512,512]{1,0:T(8,128)(2,1)S(1)} %get-tuple-element.188, bf16[512,512]{1,0:T(8,128)(2,1)S(1)} %get-tuple-element.188, bf16[512,512]{1,0:T(8,128)(2,1)S(1)} %get-tuple-element.188, ...), branch_computations={%region_0.1_spmd, %region_1.2_spmd, %region_2.3_spmd, %region_3.4_... | conditional | bytes 2097200 | solution.py:300
  105.8 12.2 %collective-permute-done.1 = bf16[512,512]{1,0:T(8,128)(2,1)} collective-permute-done((bf16[512,512]{1,0:T(8,128)(2,1)S(1)}, bf16[512,512]{1,0:T(8,128)(2,1)}, u32[]{:S(2)}, u32[]{:S(2)}) %collective-permute-start.1) | collective-permute-done | bytes 524320 | tf_op jit(solution)/shard_map/cond/branch_1_fun/ppermute | solution.py:36
  120.1 2.6 %shard_map.105 = bf16[256,8192]{1,0:T(8,128)(2,1)} custom-call(s32[6]{0:T(128)S(1)} %stack.27.place_ref, bf16[512,512]{1,0:T(8,128)(2,1)S(1)} %copy-done.9, bf16[512,512]{1,0:T(8,128)(2,1)} %collective-permute-done.19.refs_1_, bf16[512,512]{1,0:T(8,128)(2,1)} %collective-permute-done.20.refs_2_, ...), custom_call_target="tpu_custom_call", output_to_operand_aliasing={{}: (5, {})} | custom-call | flops 1 | bytes 1 | tf_op jit(solution)/shard_map/pallas_call | solution.py:123
  (67 shorter events, 29.1 us)
Async XLA Ops:
  0.6 19.0 %collective-permute-start.5 = (bf16[512,512]{1,0:T(8,128)(2,1)}, bf16[512,512]{1,0:T(8,128)(2,1)}, u32[]{:S(2)}, u32[]{:S(2)}) collective-permute-start(bf16[512,512]{1,0:T(8,128)(2,1)} %bitcast.38), channel_id=1, source_target_pairs={{0,12},{1,13},{2,14},{3,15},{4,0},{5,1},{6,2},{7,3},{8,4},{9,5},{1... | collective-permute-start | bytes 1572872 | tf_op jit(solution)/shard_map/ppermute | solution.py:27
  4.5 26.2 %collective-permute-start.6 = (bf16[512,512]{1,0:T(8,128)(2,1)}, bf16[512,512]{1,0:T(8,128)(2,1)}, u32[]{:S(2)}, u32[]{:S(2)}) collective-permute-start(bf16[512,512]{1,0:T(8,128)(2,1)} %bitcast.39), channel_id=1, source_target_pairs={{0,4},{1,5},{2,6},{3,7},{4,8},{5,9},{6,10},{7,11},{8,12},{9,13},{1... | collective-permute-start | bytes 1572872 | tf_op jit(solution)/shard_map/ppermute | solution.py:27
  11.6 19.9 %collective-permute-start.4 = (bf16[1280,512]{1,0:T(8,128)(2,1)S(1)}, bf16[1280,512]{1,0:T(8,128)(2,1)S(1)}, u32[]{:S(2)}, u32[]{:S(2)}) collective-permute-start(bf16[1280,512]{1,0:T(8,128)(2,1)S(1)} %shard_map.93), channel_id=1, source_target_pairs={{0,1},{1,0},{2,3},{3,2},{4,5},{5,4},{6,7},{7,6},{8,9},{9,8},{10,11... | collective-permute-start | bytes 3932168 | tf_op jit(solution)/shard_map/ppermute | solution.py:27
  14.8 32.3 %collective-permute-start.11 = (bf16[1024,512]{1,0:T(8,128)(2,1)S(1)}, bf16[1024,512]{1,0:T(8,128)(2,1)S(1)}, u32[]{:S(2)}, u32[]{:S(2)}) collective-permute-start(bf16[1024,512]{1,0:T(8,128)(2,1)S(1)} %shard_map.94), channel_id=1, source_target_pairs={{0,1},{1,0},{2,3},{3,2},{4,5},{5,4},{6,7},{7,6},{8,9},{9,8},{10,11... | collective-permute-start | bytes 3145736 | tf_op jit(solution)/shard_map/ppermute | solution.py:27
  32.7 14.2 %collective-permute-start.12 = (bf16[512,512]{1,0:T(8,128)(2,1)S(1)}, bf16[512,512]{1,0:T(8,128)(2,1)S(1)}, u32[]{:S(2)}, u32[]{:S(2)}) collective-permute-start(bf16[512,512]{1,0:T(8,128)(2,1)S(1)} %get-tuple-element.114), channel_id=1, source_target_pairs={{0,3},{1,2},{2,1},{3,0},{4,7},{5,6},{6,5},{7,4},{8,11},{9,10},{10,... | collective-permute-start | bytes 1572872 | tf_op jit(solution)/shard_map/ppermute | solution.py:27
  32.8 17.1 %collective-permute-start.10 = (bf16[512,512]{1,0:T(8,128)(2,1)}, bf16[512,512]{1,0:T(8,128)(2,1)}, u32[]{:S(2)}, u32[]{:S(2)}) collective-permute-start(bf16[512,512]{1,0:T(8,128)(2,1)} %collective-permute-done.5.refs_1_), channel_id=1, source_target_pairs={{0,12},{1,13},{2,14},{3,15},{4,0},{5,1},{6,2},{7,3},{8,4},{9,5},{1... | collective-permute-start | bytes 1572872 | tf_op jit(solution)/shard_map/ppermute | solution.py:27
  36.6 21.2 %collective-permute-start.9 = (bf16[512,512]{1,0:T(8,128)(2,1)S(1)}, bf16[512,512]{1,0:T(8,128)(2,1)S(1)}, u32[]{:S(2)}, u32[]{:S(2)}) collective-permute-start(bf16[512,512]{1,0:T(8,128)(2,1)S(1)} %get-tuple-element.112), channel_id=1, source_target_pairs={{0,3},{1,2},{2,1},{3,0},{4,7},{5,6},{6,5},{7,4},{8,11},{9,10},{10,... | collective-permute-start | bytes 1572872 | tf_op jit(solution)/shard_map/ppermute | solution.py:27
  38.7 21.9 %collective-permute-start.16 = (bf16[512,512]{1,0:T(8,128)(2,1)S(1)}, bf16[512,512]{1,0:T(8,128)(2,1)S(1)}, u32[]{:S(2)}, u32[]{:S(2)}) collective-permute-start(bf16[512,512]{1,0:T(8,128)(2,1)S(1)} %get-tuple-element.119), channel_id=1, source_target_pairs={{0,1},{1,0},{2,3},{3,2},{4,5},{5,4},{6,7},{7,6},{8,9},{9,8},{10,11... | collective-permute-start | bytes 1572872 | tf_op jit(solution)/shard_map/ppermute | solution.py:27
  48.4 15.1 %collective-permute-start.15 = (bf16[512,512]{1,0:T(8,128)(2,1)S(1)}, bf16[512,512]{1,0:T(8,128)(2,1)S(1)}, u32[]{:S(2)}, u32[]{:S(2)}) collective-permute-start(bf16[512,512]{1,0:T(8,128)(2,1)S(1)} %get-tuple-element.132), channel_id=1, source_target_pairs={{0,3},{1,2},{2,1},{3,0},{4,7},{5,6},{6,5},{7,4},{8,11},{9,10},{10,... | collective-permute-start | bytes 1572872 | tf_op jit(solution)/shard_map/ppermute | solution.py:27
  48.5 20.6 %collective-permute-start.14 = (bf16[512,512]{1,0:T(8,128)(2,1)S(1)}, bf16[512,512]{1,0:T(8,128)(2,1)S(1)}, u32[]{:S(2)}, u32[]{:S(2)}) collective-permute-start(bf16[512,512]{1,0:T(8,128)(2,1)S(1)} %get-tuple-element.131), channel_id=1, source_target_pairs={{0,3},{1,2},{2,1},{3,0},{4,7},{5,6},{6,5},{7,4},{8,11},{9,10},{10,... | collective-permute-start | bytes 1572872 | tf_op jit(solution)/shard_map/ppermute | solution.py:27
  50.0 20.3 %collective-permute-start.13 = (bf16[512,512]{1,0:T(8,128)(2,1)S(1)}, bf16[512,512]{1,0:T(8,128)(2,1)S(1)}, u32[]{:S(2)}, u32[]{:S(2)}) collective-permute-start(bf16[512,512]{1,0:T(8,128)(2,1)S(1)} %add_convert_fusion.2), channel_id=1, source_target_pairs={{0,4},{1,5},{2,6},{3,7},{4,8},{5,9},{6,10},{7,11},{8,12},{9,13},{1... | collective-permute-start | bytes 1572872 | tf_op jit(solution)/shard_map/ppermute | solution.py:27
  57.8 17.4 %collective-permute-start.8 = (bf16[512,512]{1,0:T(8,128)(2,1)S(1)}, bf16[512,512]{1,0:T(8,128)(2,1)S(1)}, u32[]{:S(2)}, u32[]{:S(2)}) collective-permute-start(bf16[512,512]{1,0:T(8,128)(2,1)S(1)} %bitcast.41), channel_id=1, source_target_pairs={{0,3},{1,2},{2,1},{3,0},{4,7},{5,6},{6,5},{7,4},{8,11},{9,10},{10,... | collective-permute-start | bytes 1572872 | tf_op jit(solution)/shard_map/ppermute | solution.py:27
  60.6 19.9 %collective-permute-start.17 = (bf16[512,512]{1,0:T(8,128)(2,1)}, bf16[512,512]{1,0:T(8,128)(2,1)}, u32[]{:S(2)}, u32[]{:S(2)}) collective-permute-start(bf16[512,512]{1,0:T(8,128)(2,1)} %collective-permute-done.5.refs_1_), channel_id=1, source_target_pairs={{0,3},{1,2},{2,1},{3,0},{4,7},{5,6},{6,5},{7,4},{8,11},{9,10},{10,... | collective-permute-start | bytes 1572872 | tf_op jit(solution)/shard_map/ppermute | solution.py:27
  63.5 22.5 %collective-permute-start.7 = (bf16[512,512]{1,0:T(8,128)(2,1)}, bf16[512,512]{1,0:T(8,128)(2,1)}, u32[]{:S(2)}, u32[]{:S(2)}) collective-permute-start(bf16[512,512]{1,0:T(8,128)(2,1)} %collective-permute-done.6.refs_0_), channel_id=1, source_target_pairs={{0,3},{1,2},{2,1},{3,0},{4,7},{5,6},{6,5},{7,4},{8,11},{9,10},{10,... | collective-permute-start | bytes 1572872 | tf_op jit(solution)/shard_map/ppermute | solution.py:27
  69.1 22.6 %collective-permute-start.18 = (bf16[512,512]{1,0:T(8,128)(2,1)}, bf16[512,512]{1,0:T(8,128)(2,1)}, u32[]{:S(2)}, u32[]{:S(2)}) collective-permute-start(bf16[512,512]{1,0:T(8,128)(2,1)} %collective-permute-done.10.refs_1_), channel_id=1, source_target_pairs={{0,3},{1,2},{2,1},{3,0},{4,7},{5,6},{6,5},{7,4},{8,11},{9,10},{10,... | collective-permute-start | bytes 1572872 | tf_op jit(solution)/shard_map/ppermute | solution.py:27
  71.3 28.7 %collective-permute-start.22 = (bf16[512,512]{1,0:T(8,128)(2,1)}, bf16[512,512]{1,0:T(8,128)(2,1)}, u32[]{:S(2)}, u32[]{:S(2)}) collective-permute-start(bf16[512,512]{1,0:T(8,128)(2,1)} %add_convert_fusion), channel_id=1, source_target_pairs={{0,4},{1,5},{2,6},{3,7},{4,8},{5,9},{6,10},{7,11},{8,12},{9,13},{1... | collective-permute-start | bytes 1572872 | tf_op jit(solution)/shard_map/ppermute | solution.py:27
  76.0 24.1 %collective-permute-start.23 = (bf16[512,512]{1,0:T(8,128)(2,1)}, bf16[512,512]{1,0:T(8,128)(2,1)}, u32[]{:S(2)}, u32[]{:S(2)}) collective-permute-start(bf16[512,512]{1,0:T(8,128)(2,1)} %add_convert_fusion.1), channel_id=1, source_target_pairs={{0,12},{1,13},{2,14},{3,15},{4,0},{5,1},{6,2},{7,3},{8,4},{9,5},{1... | collective-permute-start | bytes 1572872 | tf_op jit(solution)/shard_map/ppermute | solution.py:27
  83.8 16.3 %copy-start.13 = (bf16[512,512]{1,0:T(8,128)(2,1)S(1)}, bf16[512,512]{1,0:T(8,128)(2,1)}, u32[]{:S(2)}) copy-start(bf16[512,512]{1,0:T(8,128)(2,1)} %copy-done.12) | copy-start | bytes 1572868
  85.2 17.5 %copy-start.11 = (bf16[1,512,512]{2,1,0:T(8,128)(2,1)S(1)}, bf16[1,512,512]{2,1,0:T(8,128)(2,1)}, u32[]{:S(2)}) copy-start(bf16[1,512,512]{2,1,0:T(8,128)(2,1)} %param.13) | copy-start | bytes 1572868
  91.7 28.4 %collective-permute-start.20 = (bf16[512,512]{1,0:T(8,128)(2,1)}, bf16[512,512]{1,0:T(8,128)(2,1)}, u32[]{:S(2)}, u32[]{:S(2)}) collective-permute-start(bf16[512,512]{1,0:T(8,128)(2,1)} %get-tuple-element.165), channel_id=1, source_target_pairs={{0,1},{1,0},{2,3},{3,2},{4,5},{5,4},{6,7},{7,6},{8,9},{9,8},{10,11... | collective-permute-start | bytes 1572872 | tf_op jit(solution)/shard_map/ppermute | solution.py:27
  94.1 25.9 %collective-permute-start.19 = (bf16[512,512]{1,0:T(8,128)(2,1)}, bf16[512,512]{1,0:T(8,128)(2,1)}, u32[]{:S(2)}, u32[]{:S(2)}) collective-permute-start(bf16[512,512]{1,0:T(8,128)(2,1)} %get-tuple-element.164), channel_id=1, source_target_pairs={{0,1},{1,0},{2,3},{3,2},{4,5},{5,4},{6,7},{7,6},{8,9},{9,8},{10,11... | collective-permute-start | bytes 1572872 | tf_op jit(solution)/shard_map/ppermute | solution.py:27
  97.6 22.5 %collective-permute-start.21 = (bf16[512,512]{1,0:T(8,128)(2,1)}, bf16[512,512]{1,0:T(8,128)(2,1)S(1)}, u32[]{:S(2)}, u32[]{:S(2)}) collective-permute-start(bf16[512,512]{1,0:T(8,128)(2,1)} %get-tuple-element.171), channel_id=1, source_target_pairs={{0,1},{1,0},{2,3},{3,2},{4,5},{5,4},{6,7},{7,6},{8,9},{9,8},{10,11... | collective-permute-start | bytes 1572872 | tf_op jit(solution)/shard_map/ppermute | solution.py:27
  102.7 17.4 %copy-start.9 = (bf16[512,512]{1,0:T(8,128)(2,1)S(1)}, bf16[512,512]{1,0:T(8,128)(2,1)}, u32[]{:S(2)}) copy-start(bf16[512,512]{1,0:T(8,128)(2,1)} %copy-done.8) | copy-start | bytes 1572868
  104.3 13.8 %collective-permute-start.1 = (bf16[512,512]{1,0:T(8,128)(2,1)S(1)}, bf16[512,512]{1,0:T(8,128)(2,1)}, u32[]{:S(2)}, u32[]{:S(2)}) collective-permute-start(bf16[512,512]{1,0:T(8,128)(2,1)S(1)} %param.1), channel_id=1, source_target_pairs={{0,32},{16,48},{32,0},{48,16},{64,96},{80,112},{96,64},{112,80},{1... | collective-permute-start | bytes 1572872 | tf_op jit(solution)/shard_map/cond/branch_1_fun/ppermute | solution.py:36
  (11 other events, 69.2 us)

commit v2 on v1

--- a/solution.py
+++ b/solution.py
@@ -263,9 +263,6 @@
     out_rest, own_rest = run(rows_times, first, own_first, below, across)
     out_near = line(out_near)
     there_above = moved(above, "x", 1)
-    input_grad = put(
-        [(own_near, near, HERE_X), (own_rest, rest, HERE_X), (out_near, near, FIRST)]
-    )
     give_down = line(give_down)
     near_down = moved(run(added, down, give_down), "z", 1)
     give_own = line(give_own)
@@ -274,7 +271,11 @@
     there_below = moved(below, "x", 1)
     there = line(there)
     there_across = moved(across, "x", 1)
+    input_grad = put(
+        [(own_near, near, HERE_X), (own_rest, rest, HERE_X), (out_near, near, FIRST)]
+    )
     there_above = line(there_above)
+    own = run(lambda a, b: a + long(b), own, give_own)
     more_near, own_more_near = run(rows_times, first, own_first, there, there_above)
     input_grad = put([(own_more_near, near, SECOND)], input_grad)
     there_below = line(there_below)
@@ -287,7 +288,7 @@
     more_rest = moved(more_rest, "x")
     near_up = line(near_up)
     near_down = line(near_down)
-    gradient = own + long(give_own) + long(near_up) + long(near_down)
+    gradient = own + long(near_up) + long(near_down)
     new_moment = 0.9 * moment[0].astype(jnp.float32) + 0.1 * gradient
     new_second = 0.95 * second[0] + 0.05 * gradient * gradient
     weight_f = rows_here.astype(jnp.float32)

time: 123 us -> 123 us (level)
  waiting for transfers between devices: 49.8 us -> 47.2 us
  local copies, waits for them, and re-layouts: 5.89 us -> 8.07 us
    ppermute x20, waiting for transfers between devices: 37.6 us -> 35 us  [moved(): return lax.ppermute(v, ('group', 'fsdp'), pairs)]
    unnamed x28 -> x40, local copies, waits for them, and re-layouts: 5.8 us -> 7.99 us
    broadcast_in_dim x1 -> x0, other arithmetic: 1.58 us -> none  [local(): new_moment[None]]
  transfers between devices with their start and end apart: 21 -> 21, of which waited for: 9 -> 8; matrix products, arithmetic and copies ran while one was open for 7% -> 6% of each run, Pallas kernels for 14% -> 14%
where the time goes in v2:
time: 123 us; the launch traced here: 122 us
  waiting for transfers between devices  47.2 us (38%)
  starting transfers between devices  37.3 us (30%)
  Pallas kernels  20 us (16%)
  local copies, waits for them, and re-layouts  8.07 us (7%)
  other arithmetic  7.58 us (6%)
  between operations  1.73 us (1%)
    ppermute x20, starting transfers between devices, moved(): return lax.ppermute(v, ('group', 'fsdp'), pairs)  35.7 us
    ppermute x20, waiting for transfers between devices, moved(): return lax.ppermute(v, ('group', 'fsdp'), pairs)  35 us
    ppermute x1, waiting for transfers between devices, swapped(): lax.ppermute(v, 'group', [(i, i ^ 1 << bit) for i in range(lax.axis_size(...  12.2 us
    pallas_call x4, Pallas kernels, rows_times(): kernel_call(rows_kernel, (out, out), [HERE] * (2 + len(weights)), (HERE,...  9.05 us
    unnamed x40, local copies, waits for them, and re-layouts  7.99 us
    pallas_call x3, Pallas kernels, placed(): kernel_call(partial(place_kernel, blocks), jax.ShapeDtypeStruct((parts[0]...  5.68 us
    broadcast_in_dim x1, other arithmetic, local(): new_second[None]  3.27 us
    pallas_call x4, Pallas kernels, picked(): kernel_call(partial(pick_kernel, blocks), jax.ShapeDtypeStruct((count * t...  2.75 us
  transfers between devices with their start and end apart: 21, of which 8 were waited for; matrix products, arithmetic and copies ran while one was open for 6% of the time, Pallas kernels for 14%

profile of v2, /device:TPU:1, one launch (start us, length us, event | category | flops | bytes accessed | tf_op | source)
XLA Modules:
  0.0 121.9 jit_solution(17952684022935489413)
XLA Ops:
  0.6 3.9 %collective-permute-start.5 = (bf16[512,512]{1,0:T(8,128)(2,1)}, bf16[512,512]{1,0:T(8,128)(2,1)}, u32[]{:S(2)}, u32[]{:S(2)}) collective-permute-start(bf16[512,512]{1,0:T(8,128)(2,1)} %bitcast.38), channel_id=1, source_target_pairs={{0,12},{1,13},{2,14},{3,15},{4,0},{5,1},{6,2},{7,3},{8,4},{9,5},{1... | collective-permute-start | bytes 1572872 | tf_op jit(solution)/shard_map/ppermute | solution.py:27
  4.5 3.1 %collective-permute-start.6 = (bf16[512,512]{1,0:T(8,128)(2,1)}, bf16[512,512]{1,0:T(8,128)(2,1)}, u32[]{:S(2)}, u32[]{:S(2)}) collective-permute-start(bf16[512,512]{1,0:T(8,128)(2,1)} %bitcast.39), channel_id=1, source_target_pairs={{0,4},{1,5},{2,6},{3,7},{4,8},{5,9},{6,10},{7,11},{8,12},{9,13},{1... | collective-permute-start | bytes 1572872 | tf_op jit(solution)/shard_map/ppermute | solution.py:27
  7.7 2.2 %copy-done = bf16[1,256,8192]{2,1,0:T(8,128)(2,1)S(1)} copy-done((bf16[1,256,8192]{2,1,0:T(8,128)(2,1)S(1)}, bf16[1,256,8192]{2,1,0:T(8,128)(2,1)}, u32[]{:S(2)}) %copy-start) | copy-done | bytes 4194328
  11.6 2.6 %collective-permute-start.4 = (bf16[1280,512]{1,0:T(8,128)(2,1)S(1)}, bf16[1280,512]{1,0:T(8,128)(2,1)S(1)}, u32[]{:S(2)}, u32[]{:S(2)}) collective-permute-start(bf16[1280,512]{1,0:T(8,128)(2,1)S(1)} %shard_map.93), channel_id=1, source_target_pairs={{0,1},{1,0},{2,3},{3,2},{4,5},{5,4},{6,7},{7,6},{8,9},{9,8},{10,11... | collective-permute-start | bytes 3932168 | tf_op jit(solution)/shard_map/ppermute | solution.py:27
  15.8 3.8 %collective-permute-done.5.refs_1_ = bf16[512,512]{1,0:T(8,128)(2,1)} collective-permute-done((bf16[512,512]{1,0:T(8,128)(2,1)}, bf16[512,512]{1,0:T(8,128)(2,1)}, u32[]{:S(2)}, u32[]{:S(2)}) %collective-permute-start.5) | collective-permute-done | bytes 524320 | tf_op jit(solution)/shard_map/ppermute | solution.py:27
  19.6 11.1 %collective-permute-done.6.refs_0_ = bf16[512,512]{1,0:T(8,128)(2,1)} collective-permute-done((bf16[512,512]{1,0:T(8,128)(2,1)}, bf16[512,512]{1,0:T(8,128)(2,1)}, u32[]{:S(2)}, u32[]{:S(2)}) %collective-permute-start.6) | collective-permute-done | bytes 524320 | tf_op jit(solution)/shard_map/ppermute | solution.py:27
  32.8 3.8 %collective-permute-start.10 = (bf16[512,512]{1,0:T(8,128)(2,1)}, bf16[512,512]{1,0:T(8,128)(2,1)}, u32[]{:S(2)}, u32[]{:S(2)}) collective-permute-start(bf16[512,512]{1,0:T(8,128)(2,1)} %collective-permute-done.5.refs_1_), channel_id=1, source_target_pairs={{0,12},{1,13},{2,14},{3,15},{4,0},{5,1},{6,2},{7,3},{8,4},{9,5},{1... | collective-permute-start | bytes 1572872 | tf_op jit(solution)/shard_map/ppermute | solution.py:27
  38.7 2.6 %collective-permute-start.16 = (bf16[512,512]{1,0:T(8,128)(2,1)S(1)}, bf16[512,512]{1,0:T(8,128)(2,1)S(1)}, u32[]{:S(2)}, u32[]{:S(2)}) collective-permute-start(bf16[512,512]{1,0:T(8,128)(2,1)S(1)} %get-tuple-element.121), channel_id=1, source_target_pairs={{0,1},{1,0},{2,3},{3,2},{4,5},{5,4},{6,7},{7,6},{8,9},{9,8},{10,11... | collective-permute-start | bytes 1572872 | tf_op jit(solution)/shard_map/ppermute | solution.py:27
  41.2 5.7 %collective-permute-done.12 = bf16[512,512]{1,0:T(8,128)(2,1)S(1)} collective-permute-done((bf16[512,512]{1,0:T(8,128)(2,1)S(1)}, bf16[512,512]{1,0:T(8,128)(2,1)S(1)}, u32[]{:S(2)}, u32[]{:S(2)}) %collective-permute-start.12) | collective-permute-done | bytes 524320 | tf_op jit(solution)/shard_map/ppermute | solution.py:27
  50.0 3.8 %collective-permute-start.13 = (bf16[512,512]{1,0:T(8,128)(2,1)S(1)}, bf16[512,512]{1,0:T(8,128)(2,1)S(1)}, u32[]{:S(2)}, u32[]{:S(2)}) collective-permute-start(bf16[512,512]{1,0:T(8,128)(2,1)S(1)} %add_convert_fusion.2), channel_id=1, source_target_pairs={{0,4},{1,5},{2,6},{3,7},{4,8},{5,9},{6,10},{7,11},{8,12},{9,13},{1... | collective-permute-start | bytes 1572872 | tf_op jit(solution)/shard_map/ppermute | solution.py:27
  53.8 4.1 %collective-permute-done.9 = bf16[512,512]{1,0:T(8,128)(2,1)S(1)} collective-permute-done((bf16[512,512]{1,0:T(8,128)(2,1)S(1)}, bf16[512,512]{1,0:T(8,128)(2,1)S(1)}, u32[]{:S(2)}, u32[]{:S(2)}) %collective-permute-start.9) | collective-permute-done | bytes 524320 | tf_op jit(solution)/shard_map/ppermute | solution.py:27
  58.1 2.5 %shard_map.100 = (bf16[512,512]{1,0:T(8,128)(2,1)}, bf16[512,512]{1,0:T(8,128)(2,1)S(1)}) custom-call(bf16[1280,512]{1,0:T(8,128)(2,1)S(1)} %collective-permute-done.4.b_ref.v_ref.u_ref, bf16[1280,512]{1,0:T(8,128)(2,1)S(1)} %shard_map.95.a_ref.u_ref.v_ref, bf16[512,512]{1,0:T(8,128)(2,1)} %collective-permute-done.6.refs_0_, ...), custom_call_target="tpu_custom_call" | custom-call | flops 1 | bytes 1 | tf_op jit(solution)/shard_map/pallas_call | solution.py:173
  65.6 3.4 %collective-permute-done.14 = bf16[512,512]{1,0:T(8,128)(2,1)S(1)} collective-permute-done((bf16[512,512]{1,0:T(8,128)(2,1)S(1)}, bf16[512,512]{1,0:T(8,128)(2,1)S(1)}, u32[]{:S(2)}, u32[]{:S(2)}) %collective-permute-start.14) | collective-permute-done | bytes 524320 | tf_op jit(solution)/shard_map/ppermute | solution.py:27
  71.3 3.9 %collective-permute-start.22 = (bf16[512,512]{1,0:T(8,128)(2,1)}, bf16[512,512]{1,0:T(8,128)(2,1)}, u32[]{:S(2)}, u32[]{:S(2)}) collective-permute-start(bf16[512,512]{1,0:T(8,128)(2,1)} %add_convert_fusion), channel_id=1, source_target_pairs={{0,4},{1,5},{2,6},{3,7},{4,8},{5,9},{6,10},{7,11},{8,12},{9,13},{1... | collective-permute-start | bytes 1572872 | tf_op jit(solution)/shard_map/ppermute | solution.py:27
  82.7 2.3 %shard_map.102 = (bf16[512,512]{1,0:T(8,128)(2,1)}, bf16[512,512]{1,0:T(8,128)(2,1)S(1)}) custom-call(bf16[1280,512]{1,0:T(8,128)(2,1)S(1)} %collective-permute-done.4.b_ref.v_ref.u_ref, bf16[1280,512]{1,0:T(8,128)(2,1)S(1)} %shard_map.95.a_ref.u_ref.v_ref, bf16[512,512]{1,0:T(8,128)(2,1)S(1)} %copy-done.11, bf16[512,512]{1,0:T(8,128)(2,1)} %collective-permute-done.17.refs_1_), custom_call_target="tpu_custom_call" | custom-call | flops 1 | bytes 1 | tf_op jit(solution)/shard_map/pallas_call | solution.py:173
  86.4 5.2 %collective-permute-done.18.refs_1_ = bf16[512,512]{1,0:T(8,128)(2,1)} collective-permute-done((bf16[512,512]{1,0:T(8,128)(2,1)}, bf16[512,512]{1,0:T(8,128)(2,1)}, u32[]{:S(2)}, u32[]{:S(2)}) %collective-permute-start.18) | collective-permute-done | bytes 524320 | tf_op jit(solution)/shard_map/ppermute | solution.py:27
  91.7 2.5 %collective-permute-start.20 = (bf16[512,512]{1,0:T(8,128)(2,1)}, bf16[512,512]{1,0:T(8,128)(2,1)}, u32[]{:S(2)}, u32[]{:S(2)}) collective-permute-start(bf16[512,512]{1,0:T(8,128)(2,1)} %get-tuple-element.170), channel_id=1, source_target_pairs={{0,1},{1,0},{2,3},{3,2},{4,5},{5,4},{6,7},{7,6},{8,9},{9,8},{10,11... | collective-permute-start | bytes 1572872 | tf_op jit(solution)/shard_map/ppermute | solution.py:27
  94.3 2.5 %shard_map.104 = (bf16[512,512]{1,0:T(8,128)(2,1)}, bf16[512,512]{1,0:T(8,128)(2,1)S(1)}) custom-call(bf16[1280,512]{1,0:T(8,128)(2,1)S(1)} %collective-permute-done.4.b_ref.v_ref.u_ref, bf16[1280,512]{1,0:T(8,128)(2,1)S(1)} %shard_map.95.a_ref.u_ref.v_ref, bf16[512,512]{1,0:T(8,128)(2,1)} %collective-permute-done.7.refs_0_, ...), custom_call_target="tpu_custom_call" | custom-call | flops 1 | bytes 1 | tf_op jit(solution)/shard_map/pallas_call | solution.py:173
  97.6 2.5 %collective-permute-start.21 = (bf16[512,512]{1,0:T(8,128)(2,1)}, bf16[512,512]{1,0:T(8,128)(2,1)S(1)}, u32[]{:S(2)}, u32[]{:S(2)}) collective-permute-start(bf16[512,512]{1,0:T(8,128)(2,1)} %get-tuple-element.176), channel_id=1, source_target_pairs={{0,1},{1,0},{2,3},{3,2},{4,5},{5,4},{6,7},{7,6},{8,9},{9,8},{10,11... | collective-permute-start | bytes 1572872 | tf_op jit(solution)/shard_map/ppermute | solution.py:27
  100.1 3.3 %fusion.5 = (f32[1,512,512]{2,1,0:T(8,128)}, bf16[512,512]{1,0:T(8,128)(2,1)S(1)}, bf16[1,512,512]{2,1,0:T(8,128)(2,1)}) fusion(f32[1,512,512]{2,1,0:T(8,128)S(1)} %copy-done.16, bf16[512,512]{1,0:T(8,128)(2,1)} %collective-permute-done.23, f32[512,512]{1,0:T(8,128)S(1)} %convert_add_fusion.2, bf16[512,512]{1,0:T(8,128)(2,1)} %collective-permute-done.22, ...), kind=kLoop, calls=%fused_computation.15 | loop fusion | flops 5242880 | bytes 6291456 | tf_op jit(solution)/shard_map/broadcast_in_dim | solution.py:317
  103.4 13.8 %conditional.1 = (bf16[512,512]{1,0:T(8,128)(2,1)}) conditional(s32[]{:T(128)} %clamp.3, bf16[512,512]{1,0:T(8,128)(2,1)S(1)} %get-tuple-element.190, bf16[512,512]{1,0:T(8,128)(2,1)S(1)} %get-tuple-element.190, bf16[512,512]{1,0:T(8,128)(2,1)S(1)} %get-tuple-element.190, ...), branch_computations={%region_0.1_spmd, %region_1.2_spmd, %region_2.3_spmd, %region_3.4_... | conditional | bytes 2097200 | solution.py:301
  105.0 12.2 %collective-permute-done.1 = bf16[512,512]{1,0:T(8,128)(2,1)} collective-permute-done((bf16[512,512]{1,0:T(8,128)(2,1)S(1)}, bf16[512,512]{1,0:T(8,128)(2,1)}, u32[]{:S(2)}, u32[]{:S(2)}) %collective-permute-start.1) | collective-permute-done | bytes 524320 | tf_op jit(solution)/shard_map/cond/branch_1_fun/ppermute | solution.py:36
  117.2 2.0 %multiply_convert_fusion = bf16[512,512]{1,0:T(8,128)(2,1)} fusion(bf16[512,512]{1,0:T(8,128)(2,1)} %get-tuple-element.192, bf16[512,512]{1,0:T(8,128)(2,1)S(1)} %get-tuple-element.190), kind=kLoop, calls=%fused_computation.7 | loop fusion | flops 1310720 | bytes 1572864 | tf_op jit(solution)/shard_map/convert_element_type | solution.py:303
  119.2 2.6 %shard_map.105 = bf16[256,8192]{1,0:T(8,128)(2,1)} custom-call(s32[6]{0:T(128)S(1)} %stack.27.place_ref, bf16[512,512]{1,0:T(8,128)(2,1)S(1)} %copy-done.15, bf16[512,512]{1,0:T(8,128)(2,1)} %collective-permute-done.19.refs_1_, bf16[512,512]{1,0:T(8,128)(2,1)} %collective-permute-done.20.refs_2_, ...), custom_call_target="tpu_custom_call", output_to_operand_aliasing={{}: (5, {})} | custom-call | flops 1 | bytes 1 | tf_op jit(solution)/shard_map/pallas_call | solution.py:123
  (79 shorter events, 28.8 us)
Async XLA Ops:
  0.6 19.0 %collective-permute-start.5 = (bf16[512,512]{1,0:T(8,128)(2,1)}, bf16[512,512]{1,0:T(8,128)(2,1)}, u32[]{:S(2)}, u32[]{:S(2)}) collective-permute-start(bf16[512,512]{1,0:T(8,128)(2,1)} %bitcast.38), channel_id=1, source_target_pairs={{0,12},{1,13},{2,14},{3,15},{4,0},{5,1},{6,2},{7,3},{8,4},{9,5},{1... | collective-permute-start | bytes 1572872 | tf_op jit(solution)/shard_map/ppermute | solution.py:27
  4.5 26.2 %collective-permute-start.6 = (bf16[512,512]{1,0:T(8,128)(2,1)}, bf16[512,512]{1,0:T(8,128)(2,1)}, u32[]{:S(2)}, u32[]{:S(2)}) collective-permute-start(bf16[512,512]{1,0:T(8,128)(2,1)} %bitcast.39), channel_id=1, source_target_pairs={{0,4},{1,5},{2,6},{3,7},{4,8},{5,9},{6,10},{7,11},{8,12},{9,13},{1... | collective-permute-start | bytes 1572872 | tf_op jit(solution)/shard_map/ppermute | solution.py:27
  11.6 19.9 %collective-permute-start.4 = (bf16[1280,512]{1,0:T(8,128)(2,1)S(1)}, bf16[1280,512]{1,0:T(8,128)(2,1)S(1)}, u32[]{:S(2)}, u32[]{:S(2)}) collective-permute-start(bf16[1280,512]{1,0:T(8,128)(2,1)S(1)} %shard_map.93), channel_id=1, source_target_pairs={{0,1},{1,0},{2,3},{3,2},{4,5},{5,4},{6,7},{7,6},{8,9},{9,8},{10,11... | collective-permute-start | bytes 3932168 | tf_op jit(solution)/shard_map/ppermute | solution.py:27
  14.8 32.3 %collective-permute-start.11 = (bf16[1024,512]{1,0:T(8,128)(2,1)S(1)}, bf16[1024,512]{1,0:T(8,128)(2,1)S(1)}, u32[]{:S(2)}, u32[]{:S(2)}) collective-permute-start(bf16[1024,512]{1,0:T(8,128)(2,1)S(1)} %shard_map.94), channel_id=1, source_target_pairs={{0,1},{1,0},{2,3},{3,2},{4,5},{5,4},{6,7},{7,6},{8,9},{9,8},{10,11... | collective-permute-start | bytes 3145736 | tf_op jit(solution)/shard_map/ppermute | solution.py:27
  32.7 14.2 %collective-permute-start.12 = (bf16[512,512]{1,0:T(8,128)(2,1)S(1)}, bf16[512,512]{1,0:T(8,128)(2,1)S(1)}, u32[]{:S(2)}, u32[]{:S(2)}) collective-permute-start(bf16[512,512]{1,0:T(8,128)(2,1)S(1)} %get-tuple-element.116), channel_id=1, source_target_pairs={{0,3},{1,2},{2,1},{3,0},{4,7},{5,6},{6,5},{7,4},{8,11},{9,10},{10,... | collective-permute-start | bytes 1572872 | tf_op jit(solution)/shard_map/ppermute | solution.py:27
  32.8 17.1 %collective-permute-start.10 = (bf16[512,512]{1,0:T(8,128)(2,1)}, bf16[512,512]{1,0:T(8,128)(2,1)}, u32[]{:S(2)}, u32[]{:S(2)}) collective-permute-start(bf16[512,512]{1,0:T(8,128)(2,1)} %collective-permute-done.5.refs_1_), channel_id=1, source_target_pairs={{0,12},{1,13},{2,14},{3,15},{4,0},{5,1},{6,2},{7,3},{8,4},{9,5},{1... | collective-permute-start | bytes 1572872 | tf_op jit(solution)/shard_map/ppermute | solution.py:27
  36.6 21.2 %collective-permute-start.9 = (bf16[512,512]{1,0:T(8,128)(2,1)S(1)}, bf16[512,512]{1,0:T(8,128)(2,1)S(1)}, u32[]{:S(2)}, u32[]{:S(2)}) collective-permute-start(bf16[512,512]{1,0:T(8,128)(2,1)S(1)} %get-tuple-element.114), channel_id=1, source_target_pairs={{0,3},{1,2},{2,1},{3,0},{4,7},{5,6},{6,5},{7,4},{8,11},{9,10},{10,... | collective-permute-start | bytes 1572872 | tf_op jit(solution)/shard_map/ppermute | solution.py:27
  38.7 21.9 %copy-start.6 = (bf16[512,512]{1,0:T(8,128)(2,1)}, bf16[512,512]{1,0:T(8,128)(2,1)S(1)}, u32[]{:S(2)}) copy-start(bf16[512,512]{1,0:T(8,128)(2,1)S(1)} %get-tuple-element.152.refs_0_) | copy-start | bytes 1572868
  38.7 21.9 %collective-permute-start.16 = (bf16[512,512]{1,0:T(8,128)(2,1)S(1)}, bf16[512,512]{1,0:T(8,128)(2,1)S(1)}, u32[]{:S(2)}, u32[]{:S(2)}) collective-permute-start(bf16[512,512]{1,0:T(8,128)(2,1)S(1)} %get-tuple-element.121), channel_id=1, source_target_pairs={{0,1},{1,0},{2,3},{3,2},{4,5},{5,4},{6,7},{7,6},{8,9},{9,8},{10,11... | collective-permute-start | bytes 1572872 | tf_op jit(solution)/shard_map/ppermute | solution.py:27
  48.4 22.9 %copy-start.4 = (f32[512,512]{1,0:T(8,128)}, f32[512,512]{1,0:T(8,128)S(1)}, u32[]{:S(2)}) copy-start(f32[512,512]{1,0:T(8,128)S(1)} %get-tuple-element.157) | copy-start | bytes 3145732
  48.4 15.0 %collective-permute-start.15 = (bf16[512,512]{1,0:T(8,128)(2,1)S(1)}, bf16[512,512]{1,0:T(8,128)(2,1)S(1)}, u32[]{:S(2)}, u32[]{:S(2)}) collective-permute-start(bf16[512,512]{1,0:T(8,128)(2,1)S(1)} %get-tuple-element.134), channel_id=1, source_target_pairs={{0,3},{1,2},{2,1},{3,0},{4,7},{5,6},{6,5},{7,4},{8,11},{9,10},{10,... | collective-permute-start | bytes 1572872 | tf_op jit(solution)/shard_map/ppermute | solution.py:27
  48.5 20.6 %collective-permute-start.14 = (bf16[512,512]{1,0:T(8,128)(2,1)S(1)}, bf16[512,512]{1,0:T(8,128)(2,1)S(1)}, u32[]{:S(2)}, u32[]{:S(2)}) collective-permute-start(bf16[512,512]{1,0:T(8,128)(2,1)S(1)} %get-tuple-element.133), channel_id=1, source_target_pairs={{0,3},{1,2},{2,1},{3,0},{4,7},{5,6},{6,5},{7,4},{8,11},{9,10},{10,... | collective-permute-start | bytes 1572872 | tf_op jit(solution)/shard_map/ppermute | solution.py:27
  50.0 20.3 %collective-permute-start.13 = (bf16[512,512]{1,0:T(8,128)(2,1)S(1)}, bf16[512,512]{1,0:T(8,128)(2,1)S(1)}, u32[]{:S(2)}, u32[]{:S(2)}) collective-permute-start(bf16[512,512]{1,0:T(8,128)(2,1)S(1)} %add_convert_fusion.2), channel_id=1, source_target_pairs={{0,4},{1,5},{2,6},{3,7},{4,8},{5,9},{6,10},{7,11},{8,12},{9,13},{1... | collective-permute-start | bytes 1572872 | tf_op jit(solution)/shard_map/ppermute | solution.py:27
  57.8 17.4 %collective-permute-start.8 = (bf16[512,512]{1,0:T(8,128)(2,1)S(1)}, bf16[512,512]{1,0:T(8,128)(2,1)S(1)}, u32[]{:S(2)}, u32[]{:S(2)}) collective-permute-start(bf16[512,512]{1,0:T(8,128)(2,1)S(1)} %bitcast.41), channel_id=1, source_target_pairs={{0,3},{1,2},{2,1},{3,0},{4,7},{5,6},{6,5},{7,4},{8,11},{9,10},{10,... | collective-permute-start | bytes 1572872 | tf_op jit(solution)/shard_map/ppermute | solution.py:27
  60.6 21.9 %collective-permute-start.17 = (bf16[512,512]{1,0:T(8,128)(2,1)}, bf16[512,512]{1,0:T(8,128)(2,1)}, u32[]{:S(2)}, u32[]{:S(2)}) collective-permute-start(bf16[512,512]{1,0:T(8,128)(2,1)} %collective-permute-done.5.refs_1_), channel_id=1, source_target_pairs={{0,3},{1,2},{2,1},{3,0},{4,7},{5,6},{6,5},{7,4},{8,11},{9,10},{10,... | collective-permute-start | bytes 1572872 | tf_op jit(solution)/shard_map/ppermute | solution.py:27
  63.5 23.0 %collective-permute-start.7 = (bf16[512,512]{1,0:T(8,128)(2,1)}, bf16[512,512]{1,0:T(8,128)(2,1)}, u32[]{:S(2)}, u32[]{:S(2)}) collective-permute-start(bf16[512,512]{1,0:T(8,128)(2,1)} %collective-permute-done.6.refs_0_), channel_id=1, source_target_pairs={{0,3},{1,2},{2,1},{3,0},{4,7},{5,6},{6,5},{7,4},{8,11},{9,10},{10,... | collective-permute-start | bytes 1572872 | tf_op jit(solution)/shard_map/ppermute | solution.py:27
  69.1 22.6 %collective-permute-start.18 = (bf16[512,512]{1,0:T(8,128)(2,1)}, bf16[512,512]{1,0:T(8,128)(2,1)}, u32[]{:S(2)}, u32[]{:S(2)}) collective-permute-start(bf16[512,512]{1,0:T(8,128)(2,1)} %collective-permute-done.10.refs_1_), channel_id=1, source_target_pairs={{0,3},{1,2},{2,1},{3,0},{4,7},{5,6},{6,5},{7,4},{8,11},{9,10},{10,... | collective-permute-start | bytes 1572872 | tf_op jit(solution)/shard_map/ppermute | solution.py:27
  71.3 28.7 %collective-permute-start.22 = (bf16[512,512]{1,0:T(8,128)(2,1)}, bf16[512,512]{1,0:T(8,128)(2,1)}, u32[]{:S(2)}, u32[]{:S(2)}) collective-permute-start(bf16[512,512]{1,0:T(8,128)(2,1)} %add_convert_fusion), channel_id=1, source_target_pairs={{0,4},{1,5},{2,6},{3,7},{4,8},{5,9},{6,10},{7,11},{8,12},{9,13},{1... | collective-permute-start | bytes 1572872 | tf_op jit(solution)/shard_map/ppermute | solution.py:27
  76.0 24.1 %collective-permute-start.23 = (bf16[512,512]{1,0:T(8,128)(2,1)}, bf16[512,512]{1,0:T(8,128)(2,1)}, u32[]{:S(2)}, u32[]{:S(2)}) collective-permute-start(bf16[512,512]{1,0:T(8,128)(2,1)} %add_convert_fusion.1), channel_id=1, source_target_pairs={{0,12},{1,13},{2,14},{3,15},{4,0},{5,1},{6,2},{7,3},{8,4},{9,5},{1... | collective-permute-start | bytes 1572872 | tf_op jit(solution)/shard_map/ppermute | solution.py:27
  91.7 27.5 %collective-permute-start.20 = (bf16[512,512]{1,0:T(8,128)(2,1)}, bf16[512,512]{1,0:T(8,128)(2,1)}, u32[]{:S(2)}, u32[]{:S(2)}) collective-permute-start(bf16[512,512]{1,0:T(8,128)(2,1)} %get-tuple-element.170), channel_id=1, source_target_pairs={{0,1},{1,0},{2,3},{3,2},{4,5},{5,4},{6,7},{7,6},{8,9},{9,8},{10,11... | collective-permute-start | bytes 1572872 | tf_op jit(solution)/shard_map/ppermute | solution.py:27
  94.1 25.0 %collective-permute-start.19 = (bf16[512,512]{1,0:T(8,128)(2,1)}, bf16[512,512]{1,0:T(8,128)(2,1)}, u32[]{:S(2)}, u32[]{:S(2)}) collective-permute-start(bf16[512,512]{1,0:T(8,128)(2,1)} %get-tuple-element.169), channel_id=1, source_target_pairs={{0,1},{1,0},{2,3},{3,2},{4,5},{5,4},{6,7},{7,6},{8,9},{9,8},{10,11... | collective-permute-start | bytes 1572872 | tf_op jit(solution)/shard_map/ppermute | solution.py:27
  97.6 21.6 %copy-start.15 = (bf16[512,512]{1,0:T(8,128)(2,1)S(1)}, bf16[512,512]{1,0:T(8,128)(2,1)}, u32[]{:S(2)}) copy-start(bf16[512,512]{1,0:T(8,128)(2,1)} %copy-done.14) | copy-start | bytes 1572868
  97.6 21.6 %collective-permute-start.21 = (bf16[512,512]{1,0:T(8,128)(2,1)}, bf16[512,512]{1,0:T(8,128)(2,1)S(1)}, u32[]{:S(2)}, u32[]{:S(2)}) collective-permute-start(bf16[512,512]{1,0:T(8,128)(2,1)} %get-tuple-element.176), channel_id=1, source_target_pairs={{0,1},{1,0},{2,3},{3,2},{4,5},{5,4},{6,7},{7,6},{8,9},{9,8},{10,11... | collective-permute-start | bytes 1572872 | tf_op jit(solution)/shard_map/ppermute | solution.py:27
  103.4 13.8 %collective-permute-start.1 = (bf16[512,512]{1,0:T(8,128)(2,1)S(1)}, bf16[512,512]{1,0:T(8,128)(2,1)}, u32[]{:S(2)}, u32[]{:S(2)}) collective-permute-start(bf16[512,512]{1,0:T(8,128)(2,1)S(1)} %param.1), channel_id=1, source_target_pairs={{0,32},{16,48},{32,0},{48,16},{64,96},{80,112},{96,64},{112,80},{1... | collective-permute-start | bytes 1572872 | tf_op jit(solution)/shard_map/cond/branch_1_fun/ppermute | solution.py:36
  (17 other events, 95.8 us)
